TPU v7x, 256 devices: a whole 4x4x8 slice. The times are simulated.
256 devices in a mesh: dp: 128 (over z, y_lo, x, core), group: 2 (over y_hi).
Axes of the slice: x: 4, y: 4 (y_hi: 2, y_lo: 2; y = y_hi * 2 + y_lo), z: 8, core: 2. Of those that a mesh axis runs over, the one named last changes fastest.
Arguments:
- atom_feats: bfloat16 [2048, 32, 512], P(('dp', 'group')), may hold values from -6 to 6
- coords: float32 [2048, 3, 32], P(('dp', 'group')), may hold values from -6 to 6
- atom_counts: int32 [2048], P(('dp', 'group')), may hold values from 8 to 32
- positives: int32 [2048], P(('dp', 'group')), may hold values from 0 to 2047, each once
- z2: bfloat16 [2048, 128], P(('dp', 'group')), may hold values from -6 to 6
- w_qkv: bfloat16 [512, 1536], replicated, may hold values from -0.25 to 0.25
- w_out: bfloat16 [512, 512], replicated, may hold values from -0.25 to 0.25
- proj: bfloat16 [512, 128], replicated, may hold values from -0.25 to 0.25
- bias_weight: float32 [128, 64], replicated, may hold values from -2 to 36
- ln_gain: float32 [512], replicated, may hold values from 0.5 to 1.5
Outputs:
- loss: float32 [], replicated
- grad_z2: float32 [2048, 128], P(('dp', 'group'))
- grad_w_qkv: float32 [512, 1536], replicated
- grad_w_out: float32 [512, 512], replicated
- grad_proj: float32 [512, 128], replicated
- grad_bias_weight: float32 [128, 64], replicated
- grad_ln_gain: float32 [512], replicated
Inputs may be any that keep to these rules, and one draw needn't show every extreme that they name: positives is a permutation of the 2048 molecules.
All inputs are finite; a program needn't handle non-finite values.
Results may differ from a plain program's by a relative error of at most 0.014.
Values may be sent and summed in bfloat16 or wider, within the bound.
A program may use at most 128 MiB of HBM per device.

v0:
```python
import math
import jax
import jax.numpy as jnp
from jax import lax
from jax.sharding import PartitionSpec as P


def pair_distance(coords):
    offsets = coords[:, :, :, None] - coords[:, :, None, :]
    return jnp.sqrt(jnp.sum(offsets * offsets, axis=1) + 0.25)


def kernel_values(distance, kernels):
    centers = jnp.arange(kernels).astype(jnp.float32) * (12.0 / kernels)
    return jnp.exp(-(((distance[..., None] - centers) / 0.5) ** 2))


def group_split(values, width):
    return values.reshape((values.shape[0] // width, width) + values.shape[1:])


def bias_forward(distance, bias_weight):
    mol_count = distance.shape[0]
    width = math.gcd(mol_count, 8)

    def one_group(group_distance):
        basis = kernel_values(group_distance, bias_weight.shape[0])
        return jnp.einsum("mijk,kh->mhij", basis, bias_weight, precision=lax.Precision.HIGHEST)

    biased = lax.map(one_group, group_split(distance, width))
    return biased.reshape((mol_count,) + biased.shape[2:])


def bias_backward(distance, bias_slope, kernels):
    width = math.gcd(distance.shape[0], 8)

    def add_group(running, pieces):
        basis = kernel_values(pieces[0], kernels)
        return (
            running
            + jnp.einsum("mijk,mhij->kh", basis, pieces[1], precision=lax.Precision.HIGHEST),
            None,
        )

    start_sum = jnp.zeros((kernels, bias_slope.shape[1]), jnp.float32)
    summed, unused = lax.scan(
        add_group, start_sum, (group_split(distance, width), group_split(bias_slope, width))
    )
    return summed


def encode_core(params_in, pair_bias, feats, counts):
    w_qkv, w_out, proj, ln_gain = params_in
    mol_count, atom_count, model_width = feats.shape
    head_count = pair_bias.shape[1]
    head_dim = model_width // head_count
    inputs = feats.astype(jnp.float32)
    center = jnp.mean(inputs, axis=-1, keepdims=True)
    spread = jnp.mean((inputs - center) ** 2, axis=-1, keepdims=True)
    normed = ((inputs - center) * lax.rsqrt(spread + 1e-05) * ln_gain).astype(jnp.bfloat16)
    projected = jnp.dot(
        normed.reshape(mol_count * atom_count, model_width),
        w_qkv,
        preferred_element_type=jnp.float32,
    ).astype(jnp.bfloat16)
    projected = projected.reshape(mol_count, atom_count, 3, head_count, head_dim)
    query_heads = projected[:, :, 0]
    key_heads = projected[:, :, 1]
    value_heads = projected[:, :, 2]
    scores = (
        jnp.einsum("mihd,mjhd->mhij", query_heads, key_heads, preferred_element_type=jnp.float32)
        * head_dim ** (-0.5)
        + pair_bias
    )
    is_valid = jnp.arange(atom_count)[None, :] < counts[:, None]
    scores = jnp.where(is_valid[:, None, None, :], scores, -1e30)
    highest = jnp.max(scores, axis=-1, keepdims=True)
    expo = jnp.exp(scores - highest)
    attn_weights = (expo / jnp.sum(expo, axis=-1, keepdims=True)).astype(jnp.bfloat16)
    context = jnp.einsum(
        "mhij,mjhd->mihd", attn_weights, value_heads, preferred_element_type=jnp.float32
    ).astype(jnp.bfloat16)
    hidden = inputs + jnp.dot(
        context.reshape(mol_count * atom_count, model_width),
        w_out,
        preferred_element_type=jnp.float32,
    ).reshape(mol_count, atom_count, model_width)
    pooled = jnp.sum(jnp.where(is_valid[..., None], hidden, 0.0), axis=1)
    return jnp.dot(pooled.astype(jnp.bfloat16), proj, preferred_element_type=jnp.float32)


def unit_rows(values):
    inverse = lax.rsqrt(jnp.mean(values * values, axis=1, keepdims=True) + 1e-06) * values.shape[
        1
    ] ** (-0.5)
    return (values * inverse, inverse)


def unit_backward(values, inverse, grad):
    along = jnp.sum(values * grad, axis=1, keepdims=True)
    return inverse * (grad - values * along * (inverse * inverse))


def on_device(
    atom_feats, coords, atom_counts, positives, z2, w_qkv, w_out, proj, bias_weight, ln_gain
):
    distance = pair_distance(coords)
    pair_bias = bias_forward(distance, bias_weight)

    def local_encode(params_in, bias_in):
        return encode_core(params_in, bias_in, atom_feats, atom_counts)

    z3, pullback = jax.vjp(local_encode, (w_qkv, w_out, proj, ln_gain), pair_bias)
    unit, inverse = unit_rows(z3)
    z3_half = unit.astype(jnp.bfloat16)
    z2_all = lax.all_gather(z2, ("dp", "group"), axis=0, tiled=True)
    batch_rows = z2_all.shape[0]
    logits = jnp.dot(z3_half, z2_all.T, preferred_element_type=jnp.float32)
    expo = jnp.exp(logits)
    row_lse = jnp.log(jnp.sum(expo, axis=1))
    columns = jnp.arange(batch_rows)
    is_positive = positives[:, None] == columns[None, :]
    positive_score = jnp.sum(jnp.where(is_positive, logits, 0.0), axis=1)
    local_sum = jnp.sum(0.5 * row_lse - positive_score)
    col_total = lax.psum(jnp.sum(expo, axis=0), ("dp", "group"))
    col_lse = jnp.log(col_total)
    column_part = 0.5 * jnp.sum(col_lse)
    slope = (
        0.5 * jnp.exp(logits - row_lse[:, None])
        + 0.5 * jnp.exp(logits - col_lse[None, :])
        - is_positive.astype(jnp.float32)
    ).astype(jnp.bfloat16)
    grad_z2 = lax.psum_scatter(
        lax.dot_general(
            slope, z3_half, (((0,), (0,)), ((), ())), preferred_element_type=jnp.float32
        ),
        ("dp", "group"),
        scatter_dimension=0,
        tiled=True,
    )
    grad_unit = jnp.dot(slope, z2_all, preferred_element_type=jnp.float32)
    grad_z3 = unit_backward(z3, inverse, grad_unit)
    pieces, bias_slope = pullback(grad_z3)
    grad_bias = bias_backward(distance, bias_slope, bias_weight.shape[0])
    totals = lax.psum(
        (
            local_sum,
            pieces[0].astype(jnp.float32),
            pieces[1].astype(jnp.float32),
            pieces[2].astype(jnp.float32),
            grad_bias,
            pieces[3],
        ),
        ("dp", "group"),
    )
    loss = (totals[0] + column_part) / batch_rows
    return (loss, grad_z2, totals[1], totals[2], totals[3], totals[4], totals[5])


def solution(mesh):
    return jax.shard_map(
        on_device,
        mesh=mesh,
        in_specs=(
            P(("dp", "group"), None, None),
            P(("dp", "group"), None, None),
            P(("dp", "group")),
            P(("dp", "group")),
            P(("dp", "group"), None),
            P(),
            P(),
            P(),
            P(),
            P(),
        ),
        out_specs=(P(), P(("dp", "group"), None), P(), P(), P(), P(), P()),
        check_vma=False,
    )
```

profile of v0, /device:TPU:97, one launch (start us, length us, event | category | flops | bytes accessed | tf_op | source)
XLA Modules:
  0.0 1103.0 jit_solution(12725409746250518894)
XLA Ops:
  12.3 2.8 reshape.179
  15.1 3.9 fusion.58
  20.1 5.4 fusion.10
  25.5 9.2 copy.77
  34.7 7.3 fusion.60
  41.9 2.7 fusion.9
  45.2 2.3 divide_convert_fusion
  49.9 569.9 %all_gather.3 = bf16[2048,128]{1,0:T(8,128)(2,1)S(1)} all-gather(bf16[8,128]{1,0:T(8,128)(2,1)S(1)} %copy-done.25), channel_id=1, replica_groups=mesh['dp'=128,'group'=2] {'dp','group'}, dimensions={0}, use_global_device_ids=true | all-gather | bytes 526336 | tf_op jit(solution)/shard_map/all_gather | solution.py:116
  621.1 130.1 %psum.50 = f32[2048]{0:T(1024)S(1)} all-reduce(f32[2048]{0:T(1024)S(1)} %get-tuple-element.27), channel_id=1, replica_groups=mesh['dp'=128,'group'=2] {'dp','group'}, use_global_device_ids=true, to_apply=%region_12.13 | all-reduce | flops 2048 | bytes 16384 | tf_op jit(solution)/shard_map/psum | solution.py:125
  761.4 2.4 reshape.180
  763.8 5.9 fusion.21
  769.8 5.8 fusion.3
  775.7 8.8 convert_reduce_fusion
  784.5 6.1 add_select_fusion
  790.6 3.7 fusion.25
  799.9 2.7 pad_add_fusion
  802.6 5.3 copy.86
  807.9 4.3 reshape.181
  812.2 2.3 fusion.14
  816.4 8.8 copy.88
  825.2 10.3 fusion.33
  835.5 74.4 %all-reduce.4 = (f32[]{:T(128)}, f32[128,64]{0,1:T(8,128)}, f32[512]{0:T(512)}) all-reduce(f32[]{:T(128)} %get-tuple-element.52, f32[128,64]{0,1:T(8,128)S(1)} %fusion.33, f32[512]{0:T(512)S(1)} %fusion.43), channel_id=1, replica_groups=mesh['dp'=128,'group'=2] {'dp','group'}, use_global_device_ids=true, to_apply=%region_10.11 | all-reduce | flops 8705 | bytes 69640 | tf_op jit(solution)/shard_map/psum | solution.py:145
  911.2 176.8 %all-reduce.8.cloned.1.call-done = (f32[2048,128]{1,0:T(8,128)}, f32[512,1536]{1,0:T(8,128)}, f32[512,512]{1,0:T(8,128)}, f32[512,128]{1,0:T(8,128)}) async-done(((f32[2048,128]{1,0:T(8,128)}, f32[512,1536]{1,0:T(8,128)}, f32[512,512]{1,0:T(8,128)}, f32[512,128]{1,0:T(8,128)}), (f32[2048,128]{1,0:T(8,128)}, f32[512,1536]{1,0:T(8,128)}, f32[512,512]{1,0:T(8,128)}, ...) | async-done | bytes 5505040
  1089.3 3.8 copy.126
  (103 shorter events, 31.1 us)
Async XLA Ops:
  7.2 4.3 copy-start
  7.2 1080.8 %all-reduce.8.cloned.1.call-start = ((), (), s32[]{:S(2)}) async-start(), calls=%async_computation | async-start | bytes 11010048
  12.3 6.8 copy-start.27
  12.3 6.9 copy-start.23
  15.1 5.0 copy-start.26
  41.9 3.2 copy-start.1
  47.4 572.4 %copy-start.3 = (bf16[8,64,32,32]{2,3,1,0:T(8,128)(2,1)}, bf16[8,64,32,32]{2,3,1,0:T(8,128)(2,1)S(1)}, u32[]{:S(2)}) copy-start(bf16[8,64,32,32]{2,3,1,0:T(8,128)(2,1)S(1)} %divide_convert_fusion) | copy-start | bytes 3145732
  47.5 2.4 copy-start.25
  47.5 573.1 %copy-start.24 = (s32[8]{0:T(128)S(1)}, s32[8]{0:T(128)}, u32[]{:S(2)}) copy-start(s32[8]{0:T(128)} %param.13) | copy-start | bytes 100
  49.1 570.7 %copy-start.6 = (bf16[8,64,8,32]{3,2,1,0:T(8,128)(2,1)}, bf16[8,64,8,32]{3,2,1,0:T(8,128)(2,1)S(1)}, u32[]{:S(2)}) copy-start(bf16[8,64,8,32]{3,2,1,0:T(8,128)(2,1)S(1)} %convolution_convert_fusion.4) | copy-start | bytes 786436
  763.8 5.9 copy-start.8
  763.8 5.9 copy-start.10
  763.8 5.9 copy-start.16
  763.8 11.8 %slice-start = ((s8[8388608]{0:T(1024)(128)(4,1)}), s8[4194304]{0:T(1024)(128)(4,1)S(1)}, s32[]{:S(2)}) async-start(s8[8388608]{0:T(1024)(128)(4,1)} %bitcast.90), calls=%async_computation.1 | async-start | bytes 8388608
  769.8 5.9 slice-start.1
  775.6 8.8 copy-start.4
  784.5 6.1 copy-start.5
  790.6 3.7 copy-start.2
  794.4 3.6 copy-start.7
  802.6 9.6 copy-start.14
  807.9 6.6 copy-start.18
  816.4 8.8 copy-start.22
  1088.0 5.2 copy-start.17
  1089.3 4.8 copy-start.19
  (7 other events, 9.6 us)
Sparse Core Ops, SparseCore 0:
  815.9 272.0 all-reduce.7
where the time goes:
time: 1110 us; the launch traced here: 1100 us
  blocking collectives  774 us (70%)
  waiting for transfers between devices  177 us (16%)
  matrix products  54.6 us (5%)
  local copies, waits for them, and re-layouts  50.9 us (5%)
  other arithmetic  29.1 us (3%)
  between operations  17.1 us (2%)
    all_gather x1, blocking collectives, on_device(): z2_all = lax.all_gather(z2, ('dp', 'group'), axis=0, tiled=True)  570 us
    unnamed x2, waiting for transfers between devices  177 us
    psum x1, blocking collectives, on_device(): col_total = lax.psum(jnp.sum(expo, axis=0), ('dp', 'group'))  130 us
    psum x1, blocking collectives, on_device(): lax.psum((local_sum, pieces[0].astype(jnp.float32), pieces[1].astype(jnp....  74.4 us
  transfers between devices with their start and end apart: 1, of which 1 were waited for; matrix products, arithmetic and copies ran while one was open for 2% of the time, Pallas kernels for 0%

commit v1 on v0

--- a/solution.py
+++ b/solution.py
@@ -122,7 +122,7 @@
     is_positive = positives[:, None] == columns[None, :]
     positive_score = jnp.sum(jnp.where(is_positive, logits, 0.0), axis=1)
     local_sum = jnp.sum(0.5 * row_lse - positive_score)
-    col_total = lax.psum(jnp.sum(expo, axis=0), ("dp", "group"))
+    col_total = jnp.sum(lax.all_gather(jnp.sum(expo, axis=0), ("dp", "group")), axis=0)
     col_lse = jnp.log(col_total)
     column_part = 0.5 * jnp.sum(col_lse)
     slope = (

time: 1110 us -> 1730 us (1.56)
  waiting for transfers between devices: 177 us -> 917 us
  blocking collectives: 774 us -> 646 us
    all_gather x0 -> x1, waiting for transfers between devices: none -> 742 us  [on_device(): lax.all_gather(jnp.sum(expo, axis=0), ('dp', 'group'))]
    psum x1 -> x0, blocking collectives: 130 us -> none  [on_device(): col_total = lax.psum(jnp.sum(expo, axis=0), ('dp', 'group'))]
    unnamed x2 -> x3, waiting for transfers between devices: 177 us -> 176 us
  transfers between devices with their start and end apart: 1 -> 2, of which waited for: 1 -> 2; matrix products, arithmetic and copies ran while one was open for 2% -> 2% of each run, Pallas kernels for 0% -> 0%
where the time goes in v1:
time: 1730 us; the launch traced here: 1720 us
  waiting for transfers between devices  917 us (53%)
  blocking collectives  646 us (37%)
  local copies, waits for them, and re-layouts  58.6 us (3%)
  matrix products  52.8 us (3%)
  other arithmetic  29 us (2%)
    all_gather x1, waiting for transfers between devices, on_device(): lax.all_gather(jnp.sum(expo, axis=0), ('dp', 'group'))  742 us
    all_gather x1, blocking collectives, on_device(): z2_all = lax.all_gather(z2, ('dp', 'group'), axis=0, tiled=True)  570 us
    unnamed x3, waiting for transfers between devices  176 us
    psum x1, blocking collectives, on_device(): lax.psum((local_sum, pieces[0].astype(jnp.float32), pieces[1].astype(jnp....  75.7 us
  transfers between devices with their start and end apart: 2, of which 2 were waited for; matrix products, arithmetic and copies ran while one was open for 2% of the time, Pallas kernels for 0%

profile of v1, /device:TPU:97, one launch (start us, length us, event | category | flops | bytes accessed | tf_op | source)
XLA Modules:
  0.0 1720.6 jit_solution(5414974596873821139)
XLA Ops:
  12.3 2.8 reshape.181
  15.1 3.9 fusion.58
  20.1 5.4 fusion.10
  25.4 9.2 copy.77
  34.6 7.3 fusion.60
  41.9 2.7 fusion.9
  49.8 569.9 %all_gather.9 = bf16[2048,128]{1,0:T(8,128)(2,1)S(1)} all-gather(bf16[8,128]{1,0:T(8,128)(2,1)S(1)} %copy-done.26), channel_id=1, replica_groups=mesh['dp'=128,'group'=2] {'dp','group'}, dimensions={0}, use_global_device_ids=true | all-gather | bytes 526336 | tf_op jit(solution)/shard_map/all_gather | solution.py:116
  621.6 3.4 copy.87
  625.1 2.6 reshape.184
  629.1 741.8 %all-gather.3.cloned.1.call-done = f32[524288]{0:T(1024)} async-done(((f32[2048]{0:T(1024)}), f32[524288]{0:T(1024)}) %all-gather.3.cloned.1.call-update) | async-done | bytes 2097168 | tf_op jit(solution)/shard_map/all_gather | solution.py:125
  1370.9 2.7 reshape.186
  1384.1 2.4 reshape.182
  1386.5 6.0 fusion.21
  1392.5 5.8 fusion.3
  1398.5 8.8 convert_reduce_fusion
  1407.3 6.1 add_select_fusion
  1420.1 5.3 copy.86
  1425.4 4.1 reshape.183
  1429.5 2.3 fusion.14
  1433.8 8.9 copy.88
  1442.8 10.3 fusion.33
  1453.1 75.7 %all-reduce.4 = (f32[]{:T(128)}, f32[128,64]{0,1:T(8,128)}, f32[512]{0:T(512)}) all-reduce(f32[]{:T(128)} %get-tuple-element.52, f32[128,64]{0,1:T(8,128)S(1)} %fusion.33, f32[512]{0:T(512)S(1)} %fusion.43), channel_id=1, replica_groups=mesh['dp'=128,'group'=2] {'dp','group'}, use_global_device_ids=true, to_apply=%region_10.11 | all-reduce | flops 8705 | bytes 69640 | tf_op jit(solution)/shard_map/psum | solution.py:145
  1530.1 175.6 %all-reduce.8.cloned.1.call-done = (f32[2048,128]{1,0:T(8,128)}, f32[512,1536]{1,0:T(8,128)}, f32[512,512]{1,0:T(8,128)}, f32[512,128]{1,0:T(8,128)}) async-done(((f32[2048,128]{1,0:T(8,128)}, f32[512,1536]{1,0:T(8,128)}, f32[512,512]{1,0:T(8,128)}, f32[512,128]{1,0:T(8,128)}), (f32[2048,128]{1,0:T(8,128)}, f32[512,1536]{1,0:T(8,128)}, f32[512,512]{1,0:T(8,128)}, ...) | async-done | bytes 5505040
  1707.0 3.8 copy.126
  (109 shorter events, 36.7 us)
Async XLA Ops:
  7.2 4.3 copy-start
  7.2 1363.7 %all-gather.3.cloned.1.call-start = ((), (), s32[]{:S(2)}) async-start(), calls=%async_computation | async-start | bytes 2105344 | tf_op jit(solution)/shard_map/all_gather | solution.py:125
  12.3 6.7 copy-start.28
  12.3 6.8 copy-start.24
  15.1 4.9 copy-start.27
  41.9 3.2 copy-start.1
  47.4 572.4 %copy-start.3 = (bf16[8,64,32,32]{2,3,1,0:T(8,128)(2,1)}, bf16[8,64,32,32]{2,3,1,0:T(8,128)(2,1)S(1)}, u32[]{:S(2)}) copy-start(bf16[8,64,32,32]{2,3,1,0:T(8,128)(2,1)S(1)} %divide_convert_fusion) | copy-start | bytes 3145732
  47.4 573.1 %copy-start.25 = (s32[8]{0:T(128)S(1)}, s32[8]{0:T(128)}, u32[]{:S(2)}) copy-start(s32[8]{0:T(128)} %param.13) | copy-start | bytes 100
  49.1 570.7 %copy-start.6 = (bf16[8,64,8,32]{3,2,1,0:T(8,128)(2,1)}, bf16[8,64,8,32]{3,2,1,0:T(8,128)(2,1)S(1)}, u32[]{:S(2)}) copy-start(bf16[8,64,8,32]{3,2,1,0:T(8,128)(2,1)S(1)} %convolution_convert_fusion.4) | copy-start | bytes 786436
  621.5 1084.2 %all-reduce.8.cloned.1.call-start = ((), (), s32[]{:S(2)}) async-start(), calls=%async_computation.1 | async-start | bytes 11010048
  1386.5 6.0 copy-start.7
  1386.5 6.0 copy-start.9
  1386.5 6.0 copy-start.16
  1386.5 11.9 slice-start
  1392.5 5.9 slice-start.1
  1398.4 8.8 copy-start.4
  1407.3 6.1 copy-start.5
  1413.4 3.2 copy-start.2
  1420.0 9.5 copy-start.14
  1425.4 6.4 copy-start.18
  1425.4 6.4 copy-start.19
  1433.8 9.0 copy-start.23
  1705.6 5.2 copy-start.17
  1707.0 4.8 copy-start.20
  (9 other events, 14.6 us)
Sparse Core Ops, SparseCore 0:
  621.6 749.2 all-gather.2
  1433.3 272.3 all-reduce.7
